TPU v7x, 512 devices: a whole 4x8x8 slice. The times are simulated.
512 devices in a mesh: dp: 16 (over x, z_lo, core), ctx: 32 (over z_hi, y).
Axes of the slice: x: 4, y: 8, z: 8 (z_hi: 4, z_lo: 2; z = z_hi * 2 + z_lo), core: 2. Of those that a mesh axis runs over, the one named last changes fastest.
Arguments:
- queries: bfloat16 [16, 4096, 1024], P('dp', 'ctx'), may hold values from -60 to 60
- keys: bfloat16 [16, 4096, 128], P('dp', 'ctx'), may hold values from -6 to 6
- values: bfloat16 [16, 4096, 192], P('dp', 'ctx'), may hold values from -96 to 96
- features_fine: bfloat16 [16, 8192, 1536], P('dp', 'ctx'), may hold values from -6 to 6
- rc_state: bfloat16 [16, 4096, 1536], P('dp', 'ctx'), may hold values from -6 to 6
- conv_weight: float32 [5, 1536], replicated, may hold values from -2.5 to 2.5
Outputs:
- d_fine: bfloat16 [16, 8192, 1536], P('dp', 'ctx')
- d_weight: float32 [5, 1536], replicated
All inputs are finite; a program needn't handle non-finite values.
Results may differ from a plain program's by a relative error of at most 0.0085.
Values may be sent and summed in bfloat16 or wider, within the bound.
A program may use at most 64 MiB of HBM per device.

v0:
```python
import math
import jax
import jax.numpy as jnp
from jax import lax
from jax.sharding import PartitionSpec as P

HEADS = 8
KW = 5


def padded_2(cells, sides, width):
    for axis, dim in sides:
        count = lax.axis_size(axis)
        ends = count - 1
        head = lax.slice_in_dim(cells, 0, width, axis=dim)
        tail = lax.slice_in_dim(cells, cells.shape[dim] - width, cells.shape[dim], axis=dim)
        cells = jnp.concatenate(
            [
                lax.ppermute(tail, axis, [(i, (i + 1) % count) for i in range(ends)]),
                cells,
                lax.ppermute(head, axis, [((i + 1) % count, i) for i in range(ends)]),
            ],
            axis=dim,
        )
    return cells


def body(queries, keys, values, features_fine, rc_state, conv_weight):
    tok_rows = queries.shape[1]
    key_size = keys.shape[2]
    value_size = values.shape[2]
    q_heads = queries[0].reshape(tok_rows, HEADS, key_size)
    ctx_count = lax.axis_size("ctx")
    run_top = jnp.full((tok_rows, HEADS), -1e30, jnp.float32)
    key_piece = lax.all_gather(keys, "ctx", axis=1, tiled=True)
    value_piece = lax.all_gather(values, "ctx", axis=1, tiled=True)
    scores = jnp.einsum(
        "qhd,kd->qhk", q_heads, key_piece[0], preferred_element_type=jnp.float32
    ) * key_size ** (-0.5)
    new_top = jnp.maximum(run_top, jnp.max(scores, axis=-1))
    expd = jnp.exp(scores - new_top[..., None])
    new_total = jnp.sum(expd, axis=-1)
    mixed = jnp.einsum(
        "qhk,kv->qhv", expd.astype(jnp.bfloat16), value_piece[0], preferred_element_type=jnp.float32
    )
    attended = (mixed / new_total[..., None]).reshape(tok_rows, HEADS * value_size)[None]
    padded = padded_2(features_fine, (("ctx", 1),), 2)
    taps = [padded[:, k : k + 2 * tok_rows : 2, :].astype(jnp.float32) for k in range(KW)]
    coarse = conv_weight[0] * taps[0]
    for k in range(1, KW):
        coarse = coarse + conv_weight[k] * taps[k]
    slices = lax.all_to_all(rc_state, "ctx", split_axis=2, concat_axis=0, tiled=True)
    flipped = slices[::-1]
    mirrored = lax.all_to_all(flipped, "ctx", split_axis=0, concat_axis=2, tiled=True)
    grad = coarse + attended - mirrored[:, ::-1, :].astype(jnp.float32)
    gpad = padded_2(grad.astype(jnp.bfloat16), (("ctx", 1),), 1).astype(grad.dtype)
    even = (
        conv_weight[0] * gpad[:, 2:]
        + conv_weight[2] * gpad[:, 1:-1]
        + conv_weight[4] * gpad[:, :-2]
    )
    odd = conv_weight[1] * gpad[:, 2:] + conv_weight[3] * gpad[:, 1:-1]
    d_fine = (
        jnp.stack([even, odd], axis=2)
        .reshape(grad.shape[0], 2 * tok_rows, grad.shape[2])
        .astype(jnp.bfloat16)
    )
    partial_grad = jnp.stack([jnp.sum(grad * taps[k], axis=(0, 1)) for k in range(KW)])
    summed = lax.psum(partial_grad, ("dp", "ctx"))
    scale = 1.0 / math.sqrt(lax.axis_size("dp") * tok_rows * ctx_count)
    return (d_fine, summed * scale)


def solution(mesh):
    placed = (
        P("dp", "ctx", None),
        P("dp", "ctx", None),
        P("dp", "ctx", None),
        P("dp", "ctx", None),
        P("dp", "ctx", None),
        P(),
    )
    return jax.shard_map(
        body, mesh=mesh, in_specs=placed, out_specs=(P("dp", "ctx", None), P()), check_vma=False
    )
```

profile of v0, /device:TPU:184, one launch (start us, length us, event | category | flops | bytes accessed | tf_op | source)
XLA Modules:
  0.0 341.5 jit_solution(18383458230890813925)
XLA Ops:
  7.9 2.2 copy.29
  10.6 8.8 %reduce.10 = bf16[1536,128]{1,0:T(8,128)(2,1)S(1)} reduce(bf16[1536,1,128]{2,1,0:T(2,128)(2,1)S(1)} %bitcast.34, bf16[]{:T(256)} %broadcast.15), dimensions={1}, to_apply=%bitcast.29.reduce_sub_computation | reduce | bytes 786434
  20.2 13.8 %all-to-all-start = ((bf16[32,2,3072]{2,1,0:T(2,128)(2,1)}), bf16[32,2,3072]{2,1,0:T(2,128)(2,1)S(1)}, u32[]{:S(2)}, u32[]{:S(2)}) async-start(bf16[32,2,3072]{2,1,0:T(2,128)(2,1)} %reshape.84), calls=%async_computation | async-start | bytes 786432 | tf_op jit(solution)/shard_map/all_to_all | solution.py:52
  34.8 12.8 %all-to-all-done = bf16[32,2,3072]{2,1,0:T(2,128)(2,1)S(1)} async-done(((bf16[32,2,3072]{2,1,0:T(2,128)(2,1)}), bf16[32,2,3072]{2,1,0:T(2,128)(2,1)S(1)}, u32[]{:S(2)}, u32[]{:S(2)}) %all-to-all-start) | async-done | bytes 393248 | tf_op jit(solution)/shard_map/all_to_all | solution.py:52
  48.7 8.5 %all-to-all-start.1 = ((bf16[32,128,48]{1,2,0:T(8,128)(2,1)}), bf16[32,128,48]{1,2,0:T(8,128)(2,1)S(1)}, u32[]{:S(2)}, u32[]{:S(2)}) async-start(bf16[32,128,48]{1,2,0:T(8,128)(2,1)} %rev.6), calls=%async_computation.1 | async-start | bytes 786432 | tf_op jit(solution)/shard_map/all_to_all | solution.py:54
  57.5 5.5 %collective-permute-start = (bf16[1,2,1536]{1,2,0:T(8,128)(2,1)S(1)}, bf16[1,2,1536]{1,2,0:T(8,128)(2,1)}, u32[]{:S(2)}, u32[]{:S(2)}) collective-permute-start(bf16[1,2,1536]{1,2,0:T(8,128)(2,1)S(1)} %copy.24), channel_id=1, source_target_pairs={{0,1},{1,2},{2,3},{3,4},{4,5},{5,6},{6,7},{7,8},{8,9},{9,10},{10,1... | collective-permute-start | bytes 18440 | tf_op jit(solution)/shard_map/ppermute | solution.py:19
  63.3 2.1 collective-permute-start.1
  66.8 14.4 %slice.65 = bf16[1,128,1536]{1,2,0:T(8,128)(2,1)S(1)} slice(bf16[1,256,1536]{1,2,0:T(8,128)(2,1)S(1)} %copy.26), slice={[0:1:1], [0:256:2], [0:1536:1]} | slice | bytes 786432 | tf_op jit(solution)/shard_map/slice | solution.py:48
  81.2 5.9 %collective-permute-done.1 = bf16[1,2,1536]{1,2,0:T(8,128)(2,1)} collective-permute-done((bf16[1,2,1536]{1,2,0:T(8,128)(2,1)S(1)}, bf16[1,2,1536]{1,2,0:T(8,128)(2,1)}, u32[]{:S(2)}, u32[]{:S(2)}) %collective-permute-start.1) | collective-permute-done | bytes 6176 | tf_op jit(solution)/shard_map/ppermute | solution.py:21
  87.1 1.8 pad_maximum_fusion
  88.9 14.4 %slice.61 = bf16[1,128,1536]{1,2,0:T(8,128)(2,1)S(1)} slice(bf16[1,260,1536]{1,2,0:T(8,128)(2,1)S(1)} %pad_maximum_fusion), slice={[0:1:1], [0:256:2], [0:1536:1]} | slice | bytes 786432 | tf_op jit(solution)/shard_map/slice | solution.py:48
  103.3 14.4 %slice.63 = bf16[1,128,1536]{1,2,0:T(8,128)(2,1)S(1)} slice(bf16[1,260,1536]{1,2,0:T(8,128)(2,1)S(1)} %pad_maximum_fusion), slice={[0:1:1], [1:257:2], [0:1536:1]} | slice | bytes 786432 | tf_op jit(solution)/shard_map/slice | solution.py:48
  117.7 14.7 %slice.67 = bf16[1,128,1536]{1,2,0:T(8,128)(2,1)S(1)} slice(bf16[1,260,1536]{1,2,0:T(8,128)(2,1)S(1)} %pad_maximum_fusion), slice={[0:1:1], [3:259:2], [0:1536:1]} | slice | bytes 786432 | tf_op jit(solution)/shard_map/slice | solution.py:48
  132.4 15.0 %slice.69 = bf16[1,128,1536]{1,2,0:T(8,128)(2,1)} slice(bf16[1,260,1536]{1,2,0:T(8,128)(2,1)S(1)} %pad_maximum_fusion), slice={[0:1:1], [4:260:2], [0:1536:1]} | slice | bytes 786432 | tf_op jit(solution)/shard_map/slice | solution.py:48
  148.8 9.3 %multiply_reduce_fusion = (f32[128,8]{0,1:T(8,128)S(1)}, f32[128,8,4096]{2,0,1:T(8,128)}) fusion(bf16[1,4096,128]{2,1,0:T(8,128)(2,1)} %all-gather.3.cloned.1.call-done, bf16[128,8,128]{2,1,0:T(8,128)(2,1)S(1)} %bitcast.36), kind=kOutput, calls=%fused_computation.1 | convolution fusion | flops 1082129408 | bytes 18092032 | tf_op jit(solution)/shard_map/qhd,kd->qhk/dot_general | solution.py:37
  158.0 8.6 %fusion = f32[128,8]{0,1:T(8,128)S(1)} fusion(f32[128,8,4096]{2,0,1:T(8,128)} %get-tuple-element.20, f32[128,8]{0,1:T(8,128)S(1)} %broadcast_maximum_fusion), kind=kLoop, calls=%fused_computation.2 | loop fusion | flops 12581888 | bytes 16785408 | tf_op jit(solution)/shard_map/reduce_sum | solution.py:42
  166.7 29.0 %all-gather.5.cloned.1.call-done = bf16[1,4096,192]{1,2,0:T(8,128)(2,1)} async-done(((bf16[1,128,192]{1,2,0:T(8,128)(2,1)}), bf16[1,4096,192]{1,2,0:T(8,128)(2,1)}) %all-gather.5.cloned.1.call-update) | async-done | bytes 1572880 | tf_op jit(solution)/shard_map/all_gather | solution.py:36
  195.6 8.0 %fusion.7 = f32[128,8,192]{0,2,1:T(8,128)S(1)} fusion(bf16[1,4096,192]{1,2,0:T(8,128)(2,1)} %all-gather.5.cloned.1.call-done, f32[128,8,4096]{2,0,1:T(8,128)} %get-tuple-element.20, f32[128,8]{0,1:T(8,128)S(1)} %broadcast_maximum_fusion, f32[128,8]{0,1:T(8,128)S(1)} %fusion), kind=kOutput, calls=%fused_computation.19 | convolution fusion | flops 1623392256 | bytes 19144704 | tf_op jit(solution)/shard_map/qhk,kv->qhv/dot_general | solution.py:43
  203.6 2.7 fusion.22
  206.5 93.2 %psum.7 = f32[5,1536]{1,0:T(8,128)S(1)} all-reduce(f32[5,1536]{1,0:T(8,128)S(1)} %stack.38), channel_id=1, replica_groups=mesh['dp'=16,'ctx'=32] {'dp','ctx'}, use_global_device_ids=true, to_apply=%region_7.0 | all-reduce | flops 7680 | bytes 61440 | tf_op jit(solution)/shard_map/psum | solution.py:69
  299.9 6.2 %collective-permute-start.2 = (bf16[1,1,1536]{1,2,0:T(8,128)(2,1)S(1)}, bf16[1,1,1536]{1,2,0:T(8,128)(2,1)S(1)}, u32[]{:S(2)}, u32[]{:S(2)}) collective-permute-start(bf16[1,1,1536]{1,2,0:T(8,128)(2,1)S(1)} %get-tuple-element.17), channel_id=1, source_target_pairs={{0,1},{1,2},{2,3},{3,4},{4,5},{5,6},{6,7},{7,8},{8,9},{9,10},{10,1... | collective-permute-start | bytes 9224 | tf_op jit(solution)/shard_map/ppermute | solution.py:19
  306.1 1.9 collective-permute-start.3
  308.6 11.6 %collective-permute-done.2 = bf16[1,1,1536]{1,2,0:T(8,128)(2,1)S(1)} collective-permute-done((bf16[1,1,1536]{1,2,0:T(8,128)(2,1)S(1)}, bf16[1,1,1536]{1,2,0:T(8,128)(2,1)S(1)}, u32[]{:S(2)}, u32[]{:S(2)}) %collective-permute-start.2) | collective-permute-done | bytes 3104 | tf_op jit(solution)/shard_map/ppermute | solution.py:19
  320.2 10.3 %collective-permute-done.3 = bf16[1,1,1536]{1,2,0:T(8,128)(2,1)S(1)} collective-permute-done((bf16[1,1,1536]{1,2,0:T(8,128)(2,1)S(1)}, bf16[1,1,1536]{1,2,0:T(8,128)(2,1)S(1)}, u32[]{:S(2)}, u32[]{:S(2)}) %collective-permute-start.3) | collective-permute-done | bytes 3104 | tf_op jit(solution)/shard_map/ppermute | solution.py:21
  (39 shorter events, 12.2 us)
Async XLA Ops:
  7.2 141.6 %all-gather.3.cloned.1.call-start = ((), (), s32[]{:S(2)}) async-start(), calls=%async_computation.2 | async-start | bytes 1081344 | tf_op jit(solution)/shard_map/all_gather | solution.py:35
  20.2 37.0 %copy-start.1 = (bf16[1,256,1536]{2,1,0:T(8,128)(2,1)S(1)}, bf16[1,256,1536]{2,1,0:T(8,128)(2,1)}, u32[]{:S(2)}) copy-start(bf16[1,256,1536]{2,1,0:T(8,128)(2,1)} %param.9) | copy-start | bytes 2359300
  20.2 27.4 %all-to-all-start = ((bf16[32,2,3072]{2,1,0:T(2,128)(2,1)}), bf16[32,2,3072]{2,1,0:T(2,128)(2,1)S(1)}, u32[]{:S(2)}, u32[]{:S(2)}) async-start(bf16[32,2,3072]{2,1,0:T(2,128)(2,1)} %reshape.84), calls=%async_computation | async-start | bytes 786432 | tf_op jit(solution)/shard_map/all_to_all | solution.py:52
  34.0 161.6 %all-gather.5.cloned.1.call-start = ((), (), s32[]{:S(2)}) async-start(), calls=%async_computation.3 | async-start | bytes 1622016 | tf_op jit(solution)/shard_map/all_gather | solution.py:36
  34.8 30.6 %copy-start.2 = (f32[5,1536]{1,0:T(8,128)S(1)}, f32[5,1536]{1,0:T(8,128)}, u32[]{:S(2)}) copy-start(f32[5,1536]{1,0:T(8,128)} %param.11) | copy-start | bytes 92164
  48.7 98.6 %all-to-all-start.1 = ((bf16[32,128,48]{1,2,0:T(8,128)(2,1)}), bf16[32,128,48]{1,2,0:T(8,128)(2,1)S(1)}, u32[]{:S(2)}, u32[]{:S(2)}) async-start(bf16[32,128,48]{1,2,0:T(8,128)(2,1)} %rev.6), calls=%async_computation.1 | async-start | bytes 786432 | tf_op jit(solution)/shard_map/all_to_all | solution.py:54
  57.5 23.6 %collective-permute-start = (bf16[1,2,1536]{1,2,0:T(8,128)(2,1)S(1)}, bf16[1,2,1536]{1,2,0:T(8,128)(2,1)}, u32[]{:S(2)}, u32[]{:S(2)}) collective-permute-start(bf16[1,2,1536]{1,2,0:T(8,128)(2,1)S(1)} %copy.24), channel_id=1, source_target_pairs={{0,1},{1,2},{2,3},{3,4},{4,5},{5,6},{6,7},{7,8},{8,9},{9,10},{10,1... | collective-permute-start | bytes 18440 | tf_op jit(solution)/shard_map/ppermute | solution.py:19
  63.3 23.8 %collective-permute-start.1 = (bf16[1,2,1536]{1,2,0:T(8,128)(2,1)S(1)}, bf16[1,2,1536]{1,2,0:T(8,128)(2,1)}, u32[]{:S(2)}, u32[]{:S(2)}) collective-permute-start(bf16[1,2,1536]{1,2,0:T(8,128)(2,1)S(1)} %copy.25), channel_id=1, source_target_pairs={{1,0},{2,1},{3,2},{4,3},{5,4},{6,5},{7,6},{8,7},{9,8},{10,9},{11,1... | collective-permute-start | bytes 18440 | tf_op jit(solution)/shard_map/ppermute | solution.py:21
  166.7 36.9 %copy-start = (bf16[1,128,1536]{1,2,0:T(8,128)(2,1)S(1)}, bf16[1,128,1536]{1,2,0:T(8,128)(2,1)}, u32[]{:S(2)}) copy-start(bf16[1,128,1536]{1,2,0:T(8,128)(2,1)} %slice.69) | copy-start | bytes 1179652
  299.9 20.3 %collective-permute-start.2 = (bf16[1,1,1536]{1,2,0:T(8,128)(2,1)S(1)}, bf16[1,1,1536]{1,2,0:T(8,128)(2,1)S(1)}, u32[]{:S(2)}, u32[]{:S(2)}) collective-permute-start(bf16[1,1,1536]{1,2,0:T(8,128)(2,1)S(1)} %get-tuple-element.17), channel_id=1, source_target_pairs={{0,1},{1,2},{2,3},{3,4},{4,5},{5,6},{6,7},{7,8},{8,9},{9,10},{10,1... | collective-permute-start | bytes 9224 | tf_op jit(solution)/shard_map/ppermute | solution.py:19
  306.1 24.4 %collective-permute-start.3 = (bf16[1,1,1536]{1,2,0:T(8,128)(2,1)S(1)}, bf16[1,1,1536]{1,2,0:T(8,128)(2,1)S(1)}, u32[]{:S(2)}, u32[]{:S(2)}) collective-permute-start(bf16[1,1,1536]{1,2,0:T(8,128)(2,1)S(1)} %get-tuple-element.18), channel_id=1, source_target_pairs={{1,0},{2,1},{3,2},{4,3},{5,4},{6,5},{7,6},{8,7},{9,8},{10,9},{11,1... | collective-permute-start | bytes 9224 | tf_op jit(solution)/shard_map/ppermute | solution.py:21
Sparse Core Ops, SparseCore 0:
  11.2 102.2 all-gather.2
  116.5 79.0 all-gather.4
where the time goes:
time: 342 us; the launch traced here: 341 us
  blocking collectives  93.2 us (27%)
  local copies, waits for them, and re-layouts  82.9 us (24%)
  waiting for transfers between devices  70.9 us (21%)
  starting transfers between devices  38.1 us (11%)
  other arithmetic  24.9 us (7%)
  matrix products  17.2 us (5%)
  between operations  14.3 us (4%)
    psum x1, blocking collectives, body(): summed = lax.psum(partial_grad, ('dp', 'ctx'))  93.2 us
    slice x5, local copies, waits for them, and re-layouts, body(): padded[:, k:k + 2 * tok_rows:2, :].astype(jnp.float32)  72.8 us
    all_gather x1, waiting for transfers between devices, body(): value_piece = lax.all_gather(values, 'ctx', axis=1, tiled=True)  29 us
    ppermute x2, waiting for transfers between devices, padded_2(): lax.ppermute(head, axis, [((i + 1) % count, i) for i in range(ends)])  16.2 us
    all_to_all x1, starting transfers between devices, body(): lax.all_to_all(rc_state, 'ctx', split_axis=2, concat_axis=0, tiled=True)  13.8 us
    all_to_all x1, waiting for transfers between devices, body(): lax.all_to_all(rc_state, 'ctx', split_axis=2, concat_axis=0, tiled=True)  12.8 us
    ppermute x2, starting transfers between devices, padded_2(): lax.ppermute(tail, axis, [(i, (i + 1) % count) for i in range(ends)])  11.7 us
    ppermute x2, waiting for transfers between devices, padded_2(): lax.ppermute(tail, axis, [(i, (i + 1) % count) for i in range(ends)])  11.6 us
  transfers between devices with their start and end apart: 8, of which 5 were waited for; matrix products, arithmetic and copies ran while one was open for 32% of the time, Pallas kernels for 0%

commit v1 on v0

--- a/solution.py
+++ b/solution.py
@@ -66,7 +66,7 @@
         .astype(jnp.bfloat16)
     )
     partial_grad = jnp.stack([jnp.sum(grad * taps[k], axis=(0, 1)) for k in range(KW)])
-    summed = lax.psum(partial_grad, ("dp", "ctx"))
+    summed = jnp.sum(lax.all_gather(partial_grad, ("dp", "ctx")), axis=0)
     scale = 1.0 / math.sqrt(lax.axis_size("dp") * tok_rows * ctx_count)
     return (d_fine, summed * scale)
 

time: 342 us -> 1680 us (4.91)
  the two profiles are of different devices: /device:TPU:184 before, /device:TPU:194 now
where the time goes in v1:
time: 1680 us
  waiting for transfers between devices  1490 us (89%)
  local copies, waits for them, and re-layouts  83.5 us (5%)
  starting transfers between devices  35.5 us (2%)
  other arithmetic  34.8 us (2%)
  matrix products  17.2 us (1%)
    all_gather x1, waiting for transfers between devices, body(): summed = jnp.sum(lax.all_gather(partial_grad, ('dp', 'ctx')), axis=0)  1430 us
    slice x5, local copies, waits for them, and re-layouts, body(): padded[:, k:k + 2 * tok_rows:2, :].astype(jnp.float32)  72.8 us
  transfers between devices with their start and end apart: 9, of which 6 were waited for; matrix products, arithmetic and copies ran while one was open for 7% of the time, Pallas kernels for 0%

profile of v1, /device:TPU:194, one launch (start us, length us, event | category | flops | bytes accessed | tf_op | source)
XLA Modules:
  0.0 1679.3 jit_solution(1986093536371174781)
XLA Ops:
  7.9 2.2 copy.29
  10.6 8.8 reduce.11
  20.2 13.7 all-to-all-start
  34.7 15.1 all-to-all-done
  51.0 6.1 all-to-all-start.1
  57.5 4.6 collective-permute-start.1
  62.3 2.1 collective-permute-start
  65.8 14.4 slice.65
  80.9 5.6 collective-permute-done
  86.5 1.8 pad_maximum_fusion
  88.4 14.7 slice.69
  103.0 14.7 slice.67
  117.7 14.4 slice.63
  132.1 14.7 slice.61
  148.2 9.3 multiply_reduce_fusion
  157.5 8.6 fusion
  166.1 28.7 %all-gather.8.cloned.1.call-done = bf16[1,4096,192]{1,2,0:T(8,128)(2,1)} async-done(((bf16[1,128,192]{1,2,0:T(8,128)(2,1)}), bf16[1,4096,192]{1,2,0:T(8,128)(2,1)}) %all-gather.8.cloned.1.call-update) | async-done | bytes 1572880 | tf_op jit(solution)/shard_map/all_gather | solution.py:36
  194.8 8.0 fusion.7
  202.8 2.7 fusion.22
  206.5 2.4 collective-permute-start.2
  208.9 6.5 collective-permute-start.3
  215.3 11.3 collective-permute-done.2
  230.8 1431.4 %all-gather.10.cloned.1.call-done = f32[512,5,1536]{2,1,0:T(8,128)} async-done(((f32[1,5,1536]{2,1,0:T(8,128)}), f32[512,5,1536]{2,1,0:T(8,128)}) %all-gather.10.cloned.1.call-update) | async-done | bytes 15728656 | tf_op jit(solution)/shard_map/all_gather | solution.py:69
  1662.2 10.0 reduce_sum.69
  (42 shorter events, 13.6 us)
Async XLA Ops:
  7.2 141.0 %all-gather.6.cloned.1.call-start = ((), (), s32[]{:S(2)}) async-start(), calls=%async_computation.2 | async-start | bytes 1081344 | tf_op jit(solution)/shard_map/all_gather | solution.py:35
  20.2 36.9 %copy-start.1 = (bf16[1,256,1536]{2,1,0:T(8,128)(2,1)S(1)}, bf16[1,256,1536]{2,1,0:T(8,128)(2,1)}, u32[]{:S(2)}) copy-start(bf16[1,256,1536]{2,1,0:T(8,128)(2,1)} %param.9) | copy-start | bytes 2359300
  20.2 29.6 %all-to-all-start = ((bf16[32,2,3072]{2,1,0:T(2,128)(2,1)}), bf16[32,2,3072]{2,1,0:T(2,128)(2,1)S(1)}, u32[]{:S(2)}, u32[]{:S(2)}) async-start(bf16[32,2,3072]{2,1,0:T(2,128)(2,1)} %reshape.88), calls=%async_computation | async-start | bytes 786432 | tf_op jit(solution)/shard_map/all_to_all | solution.py:52
  33.9 160.9 %all-gather.8.cloned.1.call-start = ((), (), s32[]{:S(2)}) async-start(), calls=%async_computation.3 | async-start | bytes 1622016 | tf_op jit(solution)/shard_map/all_gather | solution.py:36
  34.7 29.7 %copy-start.2 = (f32[5,1536]{1,0:T(8,128)S(1)}, f32[5,1536]{1,0:T(8,128)}, u32[]{:S(2)}) copy-start(f32[5,1536]{1,0:T(8,128)} %param.11) | copy-start | bytes 92164
  51.0 95.9 %all-to-all-start.1 = ((bf16[32,128,48]{1,2,0:T(8,128)(2,1)}), bf16[32,128,48]{1,2,0:T(8,128)(2,1)S(1)}, u32[]{:S(2)}, u32[]{:S(2)}) async-start(bf16[32,128,48]{1,2,0:T(8,128)(2,1)} %rev.6), calls=%async_computation.1 | async-start | bytes 786432 | tf_op jit(solution)/shard_map/all_to_all | solution.py:54
  57.1 1605.0 %all-gather.10.cloned.1.call-start = ((), (), s32[]{:S(2)}) async-start(), calls=%async_computation.4 | async-start | bytes 25214976 | tf_op jit(solution)/shard_map/all_gather | solution.py:69
  57.5 23.4 %collective-permute-start.1 = (bf16[1,2,1536]{1,2,0:T(8,128)(2,1)S(1)}, bf16[1,2,1536]{1,2,0:T(8,128)(2,1)}, u32[]{:S(2)}, u32[]{:S(2)}) collective-permute-start(bf16[1,2,1536]{1,2,0:T(8,128)(2,1)S(1)} %copy.25), channel_id=1, source_target_pairs={{1,0},{2,1},{3,2},{4,3},{5,4},{6,5},{7,6},{8,7},{9,8},{10,9},{11,1... | collective-permute-start | bytes 18440 | tf_op jit(solution)/shard_map/ppermute | solution.py:21
  62.3 24.2 %collective-permute-start = (bf16[1,2,1536]{1,2,0:T(8,128)(2,1)S(1)}, bf16[1,2,1536]{1,2,0:T(8,128)(2,1)}, u32[]{:S(2)}, u32[]{:S(2)}) collective-permute-start(bf16[1,2,1536]{1,2,0:T(8,128)(2,1)S(1)} %copy.24), channel_id=1, source_target_pairs={{0,1},{1,2},{2,3},{3,4},{4,5},{5,6},{6,7},{7,8},{8,9},{9,10},{10,1... | collective-permute-start | bytes 18440 | tf_op jit(solution)/shard_map/ppermute | solution.py:19
  166.1 36.6 %copy-start = (bf16[1,128,1536]{1,2,0:T(8,128)(2,1)S(1)}, bf16[1,128,1536]{1,2,0:T(8,128)(2,1)}, u32[]{:S(2)}) copy-start(bf16[1,128,1536]{1,2,0:T(8,128)(2,1)} %slice.61) | copy-start | bytes 1179652
  206.5 20.1 %collective-permute-start.2 = (bf16[1,1,1536]{1,2,0:T(8,128)(2,1)S(1)}, bf16[1,1,1536]{1,2,0:T(8,128)(2,1)S(1)}, u32[]{:S(2)}, u32[]{:S(2)}) collective-permute-start(bf16[1,1,1536]{1,2,0:T(8,128)(2,1)S(1)} %get-tuple-element.17), channel_id=1, source_target_pairs={{0,1},{1,2},{2,3},{3,4},{4,5},{5,6},{6,7},{7,8},{8,9},{9,10},{10,1... | collective-permute-start | bytes 9224 | tf_op jit(solution)/shard_map/ppermute | solution.py:19
  208.9 17.7 %collective-permute-start.3 = (bf16[1,1,1536]{1,2,0:T(8,128)(2,1)S(1)}, bf16[1,1,1536]{1,2,0:T(8,128)(2,1)S(1)}, u32[]{:S(2)}, u32[]{:S(2)}) collective-permute-start(bf16[1,1,1536]{1,2,0:T(8,128)(2,1)S(1)} %get-tuple-element.18), channel_id=1, source_target_pairs={{1,0},{2,1},{3,2},{4,3},{5,4},{6,5},{7,6},{8,7},{9,8},{10,9},{11,1... | collective-permute-start | bytes 9224 | tf_op jit(solution)/shard_map/ppermute | solution.py:21
Sparse Core Ops, SparseCore 0:
  11.2 100.9 all-gather.5
  115.3 79.5 all-gather.7
  206.4 1455.6 all-gather.9
